TPU v7x, 768 devices: a whole 4x8x12 slice. The times are simulated.
768 devices in a mesh: blk: 8 (over x, y_lo), grp: 96 (over y_hi, z, core).
Axes of the slice: x: 4, y: 8 (y_hi: 4, y_lo: 2; y = y_hi * 2 + y_lo), z: 12, core: 2. Of those that a mesh axis runs over, the one named last changes fastest.
Arguments:
- features: bfloat16 [1572864, 128], P(('blk', 'grp')), may hold values from -6 to 6
- send_rows: int32 [8, 96, 8], P('blk', 'grp'), may hold values from 0 to 2047
- tile_rows: int32 [8, 96, 32], P('blk', 'grp'), may hold values from 0 to 15
- tile_cols: int32 [8, 96, 32], P('blk', 'grp'), may hold values from 0 to 47
- tile_vals: bfloat16 [8, 96, 32, 128, 128], P('blk', 'grp'), may hold values from -0.375 to 0.375
- w_self: bfloat16 [128, 256], replicated, may hold values from -0.5 to 0.5
- w_neigh: bfloat16 [128, 256], replicated, may hold values from -0.5 to 0.5
- bias: float32 [256], replicated, may hold values from -4 to 4
- grad_out: bfloat16 [1572864, 256], P(('blk', 'grp')), may hold values from -6 to 6
Outputs:
- activations: bfloat16 [1572864, 256], P(('blk', 'grp'))
- grad_self: float32 [128, 256], replicated
- grad_neigh: float32 [128, 256], replicated
All inputs are finite; a program needn't handle non-finite values.
Results may differ from a plain program's by a relative error of at most 0.015.
Values may be sent and summed in bfloat16 or wider, within the bound.
A program may use at most 32 MiB of HBM per device.

v0:
```python
import jax
import jax.numpy as jnp
from jax import lax
from jax.sharding import PartitionSpec as P

BS = 128
ROWS_DEV = 2048


def shards(features, send_rows, tile_rows, tile_cols, tile_vals, w_self, w_neigh, bias, grad_out):
    width = features.shape[1]
    own_rows = features[send_rows[0, 0]]
    shared = lax.all_gather(own_rows, ("blk", "grp"), axis=0, tiled=True)
    pre_self = jnp.dot(features, w_self, preferred_element_type=jnp.float32)
    tiles_shared = shared.reshape(-1, BS, width)
    taken = tiles_shared[tile_cols[0, 0]]
    product = jnp.einsum("tij,tjf->tif", tile_vals[0, 0], taken, preferred_element_type=jnp.float32)
    blocks = jnp.arange(ROWS_DEV // BS, dtype=jnp.int32)
    onehot = (tile_rows[0, 0][:, None] == blocks[None, :]).astype(jnp.float32)
    neigh = jnp.einsum("tr,tif->rif", onehot, product).reshape(ROWS_DEV, width).astype(jnp.bfloat16)
    pre = pre_self + jnp.dot(neigh, w_neigh, preferred_element_type=jnp.float32) + bias
    sig = jax.nn.sigmoid(pre)
    activations = (pre * sig).astype(jnp.bfloat16)
    grad_pre = (grad_out.astype(jnp.float32) * sig * (1.0 + pre * (1.0 - sig))).astype(jnp.bfloat16)
    part_self = jnp.dot(features.T, grad_pre, preferred_element_type=jnp.float32)
    part_neigh = jnp.dot(neigh.T, grad_pre, preferred_element_type=jnp.float32)
    total_self, total_neigh = lax.psum((part_self, part_neigh), ("blk", "grp"))
    nodes = ROWS_DEV * lax.axis_size("blk") * lax.axis_size("grp")
    factor = 1.0 / jnp.sqrt(jnp.float32(nodes))
    return (activations, total_self * factor, total_neigh * factor)


def solution(mesh):
    in_specs = (
        P(("blk", "grp"), None),
        P("blk", "grp", None),
        P("blk", "grp", None),
        P("blk", "grp", None),
        P("blk", "grp", None, None, None),
        P(),
        P(),
        P(),
        P(("blk", "grp"), None),
    )
    out_specs = (P(("blk", "grp"), None), P(), P())
    return jax.shard_map(shards, mesh=mesh, in_specs=in_specs, out_specs=out_specs, check_vma=False)
```

profile of v0, /device:TPU:1, one launch (start us, length us, event | category | flops | bytes accessed | tf_op | source)
XLA Modules:
  0.0 1616.3 jit_solution(13148323819265827344)
XLA Ops:
  7.2 0.0 copy-start
  7.2 0.0 all-gather.3.cloned.1.call-start
  7.2 0.7 fusion.11
  8.0 2.2 gather_fusion
  10.2 0.0 all-gather.3.cloned.1.call-update
  10.2 0.0 all-reduce.3.cloned.1.call-start
  10.3 0.7 fusion.12
  11.0 2.8 fusion.13
  13.7 1121.2 %all-gather.3.cloned.1.call-done = bf16[6144,128]{1,0:T(8,128)(2,1)} async-done(((bf16[8,128]{1,0:T(8,128)(2,1)}), bf16[6144,128]{1,0:T(8,128)(2,1)}) %all-gather.3.cloned.1.call-update) | async-done | bytes 1572880 | tf_op jit(solution)/shard_map/all_gather | solution.py:13
  1135.0 2.2 gather_fusion.1
  1137.1 0.0 copy-done
  1137.2 0.0 copy-start.3
  1137.2 0.9 fusion.6
  1138.0 0.0 copy-start.4
  1138.1 0.0 copy-start.5
  1138.1 1.0 copy.19
  1139.1 0.0 copy-start.2
  1139.1 0.0 copy-done.3
  1139.1 0.3 fusion.3
  1139.4 0.1 copy.15
  1139.5 0.0 copy-done.4
  1139.5 0.0 copy-done.5
  1139.5 1.1 copy-done.2
  1140.6 0.0 copy-start.1
  1140.6 3.5 multiply_convert_fusion
  1144.1 1.2 fusion.14
  1145.3 0.0 copy-done.1
  1145.3 1.1 convolution_bitcast_fusion
  1146.4 0.0 all-reduce.3.cloned.1.call-update
  1146.4 460.5 %all-reduce.3.cloned.1.call-done = (f32[128,256]{0,1:T(8,128)}, f32[128,256]{0,1:T(8,128)}) async-done(((f32[128,256]{0,1:T(8,128)}, f32[128,256]{0,1:T(8,128)}), (f32[128,256]{0,1:T(8,128)}, f32[128,256]{0,1:T(8,128)})) %all-reduce.3.cloned.1.call-update) | async-done | bytes 262160 | tf_op jit(solution)/shard_map/psum | solution.py:27
  1607.0 1.0 broadcast_multiply_fusion
  1608.0 0.8 copy.18
  1608.7 0.8 copy.17
  (2 shorter events, 0.0 us)
Async XLA Ops:
  7.2 1130.0 %copy-start = (bf16[1,1,32,128,128]{4,3,2,1,0:T(8,128)(2,1)S(1)}, bf16[1,1,32,128,128]{4,3,2,1,0:T(8,128)(2,1)}, u32[]{:S(2)}) copy-start(bf16[1,1,32,128,128]{4,3,2,1,0:T(8,128)(2,1)} %param.13) | copy-start | bytes 3145732
  7.2 1127.8 %all-gather.3.cloned.1.call-start = ((), (), s32[]{:S(2)}) async-start(), calls=%async_computation | async-start | bytes 1574912 | tf_op jit(solution)/shard_map/all_gather | solution.py:13
  10.2 1596.7 %all-reduce.3.cloned.1.call-start = ((), (), s32[]{:S(2)}) async-start(), calls=%async_computation.1 | async-start | bytes 524288 | tf_op jit(solution)/shard_map/psum | solution.py:27
  1137.2 1.9 copy-start.3
  1138.0 1.5 copy-start.4
  1138.1 1.5 copy-start.5
  1139.1 1.6 copy-start.2
  1140.6 4.6 copy-start.1
Sparse Core Ops, SparseCore 0:
  11.1 1123.8 all-gather.2
  1146.6 460.3 all-reduce.2
where the time goes:
time: 1620 us
  waiting for transfers between devices  1580 us (98%)
    all_gather x1, waiting for transfers between devices, shards(): shared = lax.all_gather(own_rows, ('blk', 'grp'), axis=0, tiled=True)  1120 us
    psum x1, waiting for transfers between devices, shards(): total_self, total_neigh = lax.psum((part_self, part_neigh), ('blk', 'grp'))  461 us
  transfers between devices with their start and end apart: 2, of which 2 were waited for; matrix products, arithmetic and copies ran while one was open for 0% of the time, Pallas kernels for 0%

commit v1 on v0

v1 whole, which is shorter than its diff:
```python
import functools

import jax
import jax.numpy as jnp
from jax import lax
from jax.experimental import pallas as pl
from jax.experimental.pallas import tpu as pltpu
from jax.sharding import PartitionSpec as P

MESH = pl.DeviceIdType.MESH
BS = 128
F_IN = 128
HID = 256
SEND = 8
NX = 4
YLO = 2


def ring_order(n):
    return sorted(range(1, n), key=lambda k: (min(k, n - k), k))


def kernel(
    dims,
    send_rows, tile_rows, tile_cols,
    feat_hbm, vals_hbm, ws_hbm, wn_hbm, bias_ref, gout_hbm,
    act_hbm, gs_ref, gn_ref,
    xn, w, vals, gout, act, gp, zbuf, mine, shared, prods, links,
    part, rx_core, half, rx_x, slab, rx_y, tile, rx_z, final,
    load_sem, out_sem,
    zs, zr, ys, yr, xs, xr, rs, rr, cs, cr,
    r0, r1, rxs, rxr, rys, ryr, rzs, rzr, fys, fyr, fxs, fxr, fcs, fcr,
):
    rows, tiles, nz, ny = dims
    nyh = ny // YLO
    rb = rows // BS
    chunk = nz * SEND
    blk, grp = lax.axis_index("blk"), lax.axis_index("grp")
    core = grp % 2
    z = (grp // 2) % nz
    y = (grp // (2 * nz)) * YLO + blk % YLO
    x = blk // YLO

    def at(x_, y_, z_, core_):
        return {"blk": x_ * YLO + y_ % YLO, "grp": ((y_ // YLO) * nz + z_) * 2 + core_}

    def wrap(v, n):
        return lax.rem(v + n, n)

    def copy(src, dst, send, recv, to):
        return pltpu.make_async_remote_copy(
            src_ref=src, dst_ref=dst, send_sem=send, recv_sem=recv, device_id=to, device_id_type=MESH
        )

    to_z = {k: at(x, y, wrap(z + k, nz), core) for k in range(1, nz)}
    to_y = {k: at(x, wrap(y + k, ny), z, core) for k in range(1, ny)}
    to_x = {k: at(wrap(x + k, NX), y, z, core) for k in range(1, NX)}
    twin = at(x, y, z, 1 - core)

    loads = [
        pltpu.make_async_copy(feat_hbm, xn.at[:, pl.ds(0, F_IN)], load_sem.at[0]),
        pltpu.make_async_copy(vals_hbm.at[0, 0], vals, load_sem.at[1]),
        pltpu.make_async_copy(gout_hbm, gout, load_sem.at[2]),
        pltpu.make_async_copy(ws_hbm, w.at[pl.ds(0, F_IN)], load_sem.at[3]),
        pltpu.make_async_copy(wn_hbm, w.at[pl.ds(F_IN, F_IN)], load_sem.at[4]),
    ]
    for load in loads:
        load.start()

    barrier = pltpu.get_barrier_semaphore()
    partners = [*to_z.values(), *to_y.values(), *to_x.values(), twin]
    for partner in partners:
        pl.semaphore_signal(barrier, inc=1, device_id=partner, device_id_type=MESH)

    loads[0].wait()
    picked = []
    lanes = lax.broadcasted_iota(jnp.int32, (16, F_IN), 0)
    for j in range(SEND):
        row = send_rows[0, 0, j]
        group = xn[pl.ds((row >> 4) * 16, 16), pl.ds(0, F_IN)].astype(jnp.float32)
        picked.append(jnp.sum(jnp.where(lanes == (row & 15), group, 0.0), axis=0, keepdims=True))
    mine[...] = jnp.concatenate(picked, axis=0)

    pl.semaphore_wait(barrier, len(partners))

    sent = []
    for k in reversed(ring_order(nz)):
        c = copy(mine, zbuf.at[z], zs.at[k], zr.at[k], to_z[k])
        c.start()
        sent.append(c)
    zbuf[z] = mine[...]

    loads[1].wait()
    source = lax.broadcasted_iota(jnp.int32, (BS, BS), 0)
    target = lax.broadcasted_iota(jnp.int32, (BS, BS), 1)
    wanted = ((target % 64) // SEND) * (2 * SEND) + (target // 64) * SEND + target % SEND
    order = (source == wanted).astype(jnp.bfloat16)

    @pl.loop(0, tiles // 4)
    def _(i):
        block = vals[pl.ds(i * 4, 4)].reshape(4 * BS, BS)
        moved = jnp.dot(block, order, preferred_element_type=jnp.float32)
        vals[pl.ds(i * 4, 4)] = moved.astype(jnp.bfloat16).reshape(4, BS, BS)

    def latest(r, end):
        return lax.fori_loop(
            0, end, lambda s, best: jnp.maximum(best, (tile_rows[0, 0, s] == r).astype(jnp.int32) * (s + 1)), jnp.int32(0)
        )

    @pl.loop(0, tiles)
    def _(t):
        links[t] = latest(tile_rows[0, 0, t], t)

    @pl.loop(0, rb)
    def _(r):
        links[64 + r] = latest(r, tiles)

    prods[0] = jnp.zeros((BS, F_IN), jnp.float32)

    def place(x_, y_):
        return pl.ds(pl.multiple_of(((x_ * YLO + y_ % YLO) * nyh + y_ // YLO) * chunk, 32), chunk)

    def slab_of(x_):
        return pl.ds(pl.multiple_of(x_ * (ny * chunk), 32), ny * chunk)

    for k in ring_order(nz):
        copy(mine, zbuf.at[wrap(z - k, nz)], zs.at[k], zr.at[k], to_z[k]).wait_recv()
    shared[core, place(x, y)] = zbuf[...].reshape(chunk, F_IN).astype(jnp.bfloat16)

    def send_x(k):
        where = shared.at[core, place(x, wrap(y - k, ny))]
        for i, step in enumerate((1, NX - 1)):
            c = copy(where, where, xs.at[i, k], xr.at[i, k], to_x[step])
            c.start()
            sent.append(c)

    send_x(0)
    own = shared.at[core, place(x, y)]
    for k in reversed(ring_order(ny)):
        c = copy(own, own, ys.at[k], yr.at[k], to_y[k])
        c.start()
        sent.append(c)
    for k in ring_order(ny):
        where = shared.at[core, place(x, wrap(y - k, ny))]
        copy(where, where, ys.at[k], yr.at[k], to_y[k]).wait_recv()
        send_x(k)

    def to_twin(i, x_):
        where = shared.at[core, slab_of(x_)]
        c = copy(where, where, cs.at[i], cr.at[i], twin)
        c.start()
        sent.append(c)

    to_twin(0, x)
    for k in (0, *ring_order(ny)):
        for i, step in enumerate((1, NX - 1)):
            where = shared.at[core, place(wrap(x - step, NX), wrap(y - k, ny))]
            copy(where, where, xs.at[i, k], xr.at[i, k], to_x[step]).wait_recv()
            if (k < ny // 2) == (i == 0):
                c = copy(where, where, rs.at[k], rr.at[k], to_x[step])
                c.start()
                sent.append(c)
    to_twin(1, wrap(x - 1, NX))
    to_twin(2, wrap(x + 1, NX))
    for k in (0, *ring_order(ny)):
        where = shared.at[core, place(wrap(x + 2, NX), wrap(y - k, ny))]
        copy(where, where, rs.at[k], rr.at[k], to_x[1]).wait_recv()
    to_twin(3, wrap(x + 2, NX))
    for i, x_ in enumerate((x, wrap(x - 1, NX), wrap(x + 1, NX), wrap(x + 2, NX))):
        where = shared.at[1 - core, slab_of(x_)]
        copy(where, where, cs.at[i], cr.at[i], twin).wait_recv()

    for t in range(tiles):
        here = pl.ds(tile_cols[0, 0, t] * 64, 64)
        taken = jnp.concatenate([shared[0, here], shared[1, here]], axis=0)
        prods[t + 1] = jnp.dot(vals[t], taken, preferred_element_type=jnp.float32)

    @pl.loop(0, tiles)
    def _(t):
        prods[t + 1] = prods[t + 1] + prods[links[t]]

    for load in loads[2:]:
        load.wait()
    step_rows = 2 * BS

    @pl.loop(0, rows // step_rows)
    def _(i):
        here = pl.ds(pl.multiple_of(i * step_rows, step_rows), step_rows)
        neigh = jnp.concatenate([prods[links[64 + 2 * i]], prods[links[65 + 2 * i]]], axis=0)
        xn[here, pl.ds(F_IN, F_IN)] = neigh.astype(jnp.bfloat16)
        pre = jnp.dot(xn[here], w[...], preferred_element_type=jnp.float32) + bias_ref[...]
        sig = jax.nn.sigmoid(pre)
        act[here] = (pre * sig).astype(jnp.bfloat16)
        gp[here] = (gout[here].astype(jnp.float32) * sig * (1.0 + pre * (1.0 - sig))).astype(jnp.bfloat16)

    act_out = pltpu.make_async_copy(act, act_hbm, out_sem)
    act_out.start()
    grads = lax.dot_general(xn[...], gp[...], (((0,), (0,)), ((), ())), preferred_element_type=jnp.float32)
    for s in range(2):
        for m in range(32):
            r, l = F_IN * s + 8 * (m // 2), 128 * (m % 2)
            part[s, m] = grads[r:r + 8, l:l + 128]

    c = copy(part.at[1 - core], rx_core, r0, r1, twin)
    c.start()
    sent.append(c)
    c.wait_recv()
    half[...] = part[core] + rx_core[...]
    per = 32 // NX
    for k in (2, 1, 3):
        c = copy(half.at[pl.ds(wrap(x + k, NX) * per, per)], rx_x.at[k], rxs.at[k], rxr.at[k], to_x[k])
        c.start()
        sent.append(c)
    for k in (1, 3, 2):
        copy(half.at[pl.ds(0, per)], rx_x.at[k], rxs.at[k], rxr.at[k], to_x[k]).wait_recv()
    slab[...] = half[pl.ds(x * per, per)] + rx_x[1] + rx_x[2] + rx_x[3]
    each = per // ny
    for k in reversed(ring_order(ny)):
        c = copy(slab.at[pl.ds(wrap(y + k, ny) * each, each)], rx_y.at[k], rys.at[k], ryr.at[k], to_y[k])
        c.start()
        sent.append(c)
    total = slab[pl.ds(y * each, each)]
    for k in ring_order(ny):
        copy(slab.at[pl.ds(0, each)], rx_y.at[k], rys.at[k], ryr.at[k], to_y[k]).wait_recv()
        total = total + rx_y[k]
    tile[...] = total
    for k in reversed(ring_order(nz)):
        c = copy(tile, rx_z.at[z], rzs.at[k], rzr.at[k], to_z[k])
        c.start()
        sent.append(c)
    rx_z[z] = total
    for k in ring_order(nz):
        copy(tile, rx_z.at[wrap(z - k, nz)], rzs.at[k], rzr.at[k], to_z[k]).wait_recv()
    total = rx_z[0]
    for k in range(1, nz):
        total = total + rx_z[k]
    nodes = rows * lax.axis_size("blk") * lax.axis_size("grp")
    factor = 1.0 / jnp.sqrt(jnp.float32(nodes))

    def share(x_, y_):
        return pl.ds(x_ * per + y_ * each, each)

    final[core, share(x, y)] = total * factor
    own = final.at[core, share(x, y)]
    for k in reversed(ring_order(ny)):
        c = copy(own, own, fys.at[k], fyr.at[k], to_y[k])
        c.start()
        sent.append(c)
    for k in ring_order(ny):
        where = final.at[core, share(x, wrap(y - k, ny))]
        copy(where, where, fys.at[k], fyr.at[k], to_y[k]).wait_recv()
    own = final.at[core, pl.ds(x * per, per)]
    for k in (2, 1, 3):
        c = copy(own, own, fxs.at[k], fxr.at[k], to_x[k])
        c.start()
        sent.append(c)
    c = copy(own, own, fcs.at[0], fcr.at[0], twin)
    c.start()
    sent.append(c)
    for k in (1, 3, 2):
        where = final.at[core, pl.ds(wrap(x - k, NX) * per, per)]
        copy(where, where, fxs.at[k], fxr.at[k], to_x[k]).wait_recv()
        c = copy(where, where, fcs.at[k], fcr.at[k], twin)
        c.start()
        sent.append(c)
    for k in range(NX):
        where = final.at[1 - core, pl.ds(wrap(x - k, NX) * per, per)]
        copy(where, where, fcs.at[k], fcr.at[k], twin).wait_recv()
    for s, ref in enumerate((gs_ref, gn_ref)):
        for m in range(32):
            ref[8 * (m // 2):8 * (m // 2) + 8, 128 * (m % 2):128 * (m % 2) + 128] = final[s, m]
    for c in sent:
        c.wait_send()
    act_out.wait()


def shards(mesh_shape, features, send_rows, tile_rows, tile_cols, tile_vals, w_self, w_neigh, bias, grad_out):
    rows = features.shape[0]
    tiles = tile_vals.shape[2]
    nx_ylo, rest = mesh_shape
    nyh = 4
    nz = rest // (2 * nyh)
    ny = nyh * YLO
    ndev = nx_ylo * rest
    per = 32 // NX
    each = per // ny
    bf16, f32 = jnp.bfloat16, jnp.float32
    dma = pltpu.SemaphoreType.DMA
    smem = pl.BlockSpec(memory_space=pltpu.SMEM)
    anywhere = pl.BlockSpec(memory_space=pl.ANY)
    vmem = pl.BlockSpec(memory_space=pltpu.VMEM)
    return pl.pallas_call(
        functools.partial(kernel, (rows, tiles, nz, ny)),
        out_shape=(
            jax.ShapeDtypeStruct((rows, HID), bf16),
            jax.ShapeDtypeStruct((F_IN, HID), f32),
            jax.ShapeDtypeStruct((F_IN, HID), f32),
        ),
        in_specs=[smem, smem, smem, anywhere, anywhere, anywhere, anywhere, vmem, anywhere],
        out_specs=(anywhere, vmem, vmem),
        scratch_shapes=[
            pltpu.VMEM((rows, 2 * F_IN), bf16),
            pltpu.VMEM((2 * F_IN, HID), bf16),
            pltpu.VMEM((tiles, BS, BS), bf16),
            pltpu.VMEM((rows, HID), bf16),
            pltpu.VMEM((rows, HID), bf16),
            pltpu.VMEM((rows, HID), bf16),
            pltpu.VMEM((nz, SEND, F_IN), f32),
            pltpu.VMEM((SEND, F_IN), f32),
            pltpu.VMEM((2, ndev // 2 * SEND, F_IN), bf16),
            pltpu.VMEM((tiles + 1, BS, F_IN), f32),
            pltpu.SMEM((128,), jnp.int32),
            pltpu.VMEM((2, 32, 8, 128), f32),
            pltpu.VMEM((32, 8, 128), f32),
            pltpu.VMEM((32, 8, 128), f32),
            pltpu.VMEM((NX, per, 8, 128), f32),
            pltpu.VMEM((per, 8, 128), f32),
            pltpu.VMEM((ny, each, 8, 128), f32),
            pltpu.VMEM((each, 8, 128), f32),
            pltpu.VMEM((nz, each, 8, 128), f32),
            pltpu.VMEM((2, 32, 8, 128), f32),
            dma((5,)), dma,
            dma((nz,)), dma((nz,)), dma((ny,)), dma((ny,)), dma((2, ny)), dma((2, ny)),
            dma((ny,)), dma((ny,)), dma((4,)), dma((4,)),
            dma, dma, dma((NX,)), dma((NX,)), dma((ny,)), dma((ny,)), dma((nz,)), dma((nz,)),
            dma((ny,)), dma((ny,)), dma((NX,)), dma((NX,)), dma((NX,)), dma((NX,)),
        ],
        compiler_params=pltpu.CompilerParams(
            collective_id=0, has_side_effects=True, vmem_limit_bytes=40 * 1024 * 1024
        ),
    )(send_rows, tile_rows, tile_cols, features, tile_vals, w_self, w_neigh, bias.reshape(1, HID), grad_out)


def solution(mesh):
    in_specs = (
        P(("blk", "grp"), None),
        P("blk", "grp", None),
        P("blk", "grp", None),
        P("blk", "grp", None),
        P("blk", "grp", None, None, None),
        P(),
        P(),
        P(),
        P(("blk", "grp"), None),
    )
    out_specs = (P(("blk", "grp"), None), P(), P())
    body = functools.partial(shards, (mesh.shape["blk"], mesh.shape["grp"]))
    return jax.shard_map(body, mesh=mesh, in_specs=in_specs, out_specs=out_specs, check_vma=False)
```

time: 1620 us -> 88.6 us (0.05)
  waiting for transfers between devices: 1580 us -> 0 us
  Pallas kernels: 0 us -> 78.2 us
    all_gather x1 -> x0, waiting for transfers between devices: 1120 us -> none  [shards(): shared = lax.all_gather(own_rows, ('blk', 'grp'), axis=0, tiled=True)]
    psum x1 -> x0, waiting for transfers between devices: 461 us -> none  [shards(): total_self, total_neigh = lax.psum((part_self, part_neigh), ('blk', 'grp'))]
    pallas_call x0 -> x1, Pallas kernels: none -> 78.2 us  [shards(): pl.pallas_call(functools.partial(kernel, (rows, tiles, nz, ny)), out_shap...]
  transfers between devices with their start and end apart: 2 -> 0, of which waited for: 2 -> 0; matrix products, arithmetic and copies ran while one was open for 0% -> 0% of each run, Pallas kernels for 0% -> 0%
where the time goes in v1:
time: 88.6 us; the launch traced here: 88.3 us
  Pallas kernels  78.2 us (88%)
  local copies, waits for them, and re-layouts  9.43 us (11%)
    pallas_call x1, Pallas kernels, shards(): pl.pallas_call(functools.partial(kernel, (rows, tiles, nz, ny)), out_shap...  78.2 us
    unnamed x21, local copies, waits for them, and re-layouts  9.43 us

profile of v1, /device:TPU:1, one launch (start us, length us, event | category | flops | bytes accessed | tf_op | source)
XLA Modules:
  0.0 88.3 jit_solution(1881652184468396143)
XLA Ops:
  0.6 0.0 copy-start.5
  0.6 0.0 copy-start.6
  0.7 0.7 copy-done.5
  1.3 0.0 copy-done.6
  1.3 0.0 copy-start
  1.3 1.2 %copy-done = bf16[1,1,32,128,128]{4,3,2,1,0:T(8,128)(2,1)S(1)} copy-done((bf16[1,1,32,128,128]{4,3,2,1,0:T(8,128)(2,1)S(1)}, bf16[1,1,32,128,128]{4,3,2,1,0:T(8,128)(2,1)}, u32[]{:S(2)}) %copy-start) | copy-done | bytes 1048600
  2.5 0.0 copy-start.1
  2.5 1.2 %copy-done.1 = bf16[2048,256]{1,0:T(8,128)(2,1)S(1)} copy-done((bf16[2048,256]{1,0:T(8,128)(2,1)S(1)}, bf16[2048,256]{1,0:T(8,128)(2,1)}, u32[]{:S(2)}) %copy-start.1) | copy-done | bytes 1048600
  3.8 0.0 copy-start.2
  3.8 1.0 %copy-done.2 = bf16[2048,128]{1,0:T(8,128)(2,1)S(1)} copy-done((bf16[2048,128]{1,0:T(8,128)(2,1)S(1)}, bf16[2048,128]{1,0:T(8,128)(2,1)}, u32[]{:S(2)}) %copy-start.2) | copy-done | bytes 524312
  4.8 0.0 copy-start.3
  4.8 0.8 copy-done.3
  5.6 0.0 copy-start.4
  5.7 0.8 copy-done.4
  6.5 0.0 copy-start.7
  6.5 0.7 copy-done.7
  7.1 0.0 copy-start.8
  7.1 0.7 copy-done.8
  7.8 78.2 %shard_map.112 = (bf16[2048,256]{1,0:T(8,128)(2,1)S(1)}, f32[128,256]{1,0:T(8,128)S(1)}, f32[128,256]{1,0:T(8,128)S(1)}) custom-call(s32[1,1,8]{2,1,0:T(1,128)S(1)} %copy-done.6, s32[1,1,32]{2,1,0:T(1,128)S(1)} %copy-done.7, s32[1,1,32]{2,1,0:T(1,128)S(1)} %copy-done.8, bf16[2048,128]{1,0:T(8,128)(2,1)S(1)} %copy-done.2, ...), custom_call_target="tpu_custom_call" | custom-call | tf_op jit(solution)/shard_map/pallas_call | solution.py:292
  86.0 1.0 %copy.15 = bf16[2048,256]{1,0:T(8,128)(2,1)} copy(bf16[2048,256]{1,0:T(8,128)(2,1)S(1)} %get-tuple-element.6) | data formatting | bytes 2097152
  86.9 0.7 copy.16
  87.6 0.7 copy.17
Async XLA Ops:
  0.6 0.7 copy-start.5
  0.6 0.7 copy-start.6
  1.3 1.2 %copy-start = (bf16[1,1,32,128,128]{4,3,2,1,0:T(8,128)(2,1)S(1)}, bf16[1,1,32,128,128]{4,3,2,1,0:T(8,128)(2,1)}, u32[]{:S(2)}) copy-start(bf16[1,1,32,128,128]{4,3,2,1,0:T(8,128)(2,1)} %vals_hbm.1) | copy-start | bytes 3145732
  2.5 1.2 %copy-start.1 = (bf16[2048,256]{1,0:T(8,128)(2,1)S(1)}, bf16[2048,256]{1,0:T(8,128)(2,1)}, u32[]{:S(2)}) copy-start(bf16[2048,256]{1,0:T(8,128)(2,1)} %gout_hbm.1) | copy-start | bytes 3145732
  3.8 1.0 %copy-start.2 = (bf16[2048,128]{1,0:T(8,128)(2,1)S(1)}, bf16[2048,128]{1,0:T(8,128)(2,1)}, u32[]{:S(2)}) copy-start(bf16[2048,128]{1,0:T(8,128)(2,1)} %feat_hbm.1) | copy-start | bytes 1572868
  4.8 0.8 copy-start.3
  5.6 0.8 copy-start.4
  6.5 0.7 copy-start.7
  7.1 0.7 copy-start.8

commit v2 on v1

v2 whole, which is shorter than its diff:
```python
import functools

import jax
import jax.numpy as jnp
from jax import lax
from jax.experimental import pallas as pl
from jax.experimental.pallas import tpu as pltpu
from jax.sharding import PartitionSpec as P

MESH = pl.DeviceIdType.MESH
BS = 128
F_IN = 128
HID = 256
SEND = 8
NX = 4
YLO = 2


def ring_order(n):
    return sorted(range(1, n), key=lambda k: (min(k, n - k), k))


def kernel(
    dims,
    send_hbm, trows_hbm, tcols_hbm,
    feat_hbm, vals_hbm, ws_hbm, wn_hbm, bias_hbm, gout_hbm,
    act, gs_ref, gn_ref,
    send_rows, tile_rows, tile_cols, bias_ref, xn, w, vals, gout, gp, zbuf, mine, shared, prods, links,
    part, rx_core, half, rx_xy, tile, rx_z, final,
    load_sem,
    zs, zr, ys, yr, xs, xr, rs, rr, cs, cr,
    r0, r1, rxs, rxr, rzs, rzr, fxs, fxr, fcs, fcr,
):
    rows, tiles, nz, ny = dims
    nyh = ny // YLO
    rb = rows // BS
    chunk = nz * SEND
    blk, grp = lax.axis_index("blk"), lax.axis_index("grp")
    core = grp % 2
    z = (grp // 2) % nz
    y = (grp // (2 * nz)) * YLO + blk % YLO
    x = blk // YLO

    def at(x_, y_, z_, core_):
        return {"blk": x_ * YLO + y_ % YLO, "grp": ((y_ // YLO) * nz + z_) * 2 + core_}

    def wrap(v, n):
        return lax.rem(v + n, n)

    def copy(src, dst, send, recv, to):
        return pltpu.make_async_remote_copy(
            src_ref=src, dst_ref=dst, send_sem=send, recv_sem=recv, device_id=to, device_id_type=MESH
        )

    to_z = {k: at(x, y, wrap(z + k, nz), core) for k in range(1, nz)}
    to_y = {k: at(x, wrap(y + k, ny), z, core) for k in range(1, ny)}
    to_x = {k: at(wrap(x + k, NX), y, z, core) for k in (1, NX - 1)}
    twin = at(x, y, z, 1 - core)

    loads = [
        pltpu.make_async_copy(feat_hbm, xn.at[:, pl.ds(0, F_IN)], load_sem.at[0]),
        pltpu.make_async_copy(vals_hbm.at[0, 0], vals, load_sem.at[1]),
        pltpu.make_async_copy(gout_hbm, gout, load_sem.at[2]),
        pltpu.make_async_copy(ws_hbm, w.at[pl.ds(0, F_IN)], load_sem.at[3]),
        pltpu.make_async_copy(wn_hbm, w.at[pl.ds(F_IN, F_IN)], load_sem.at[4]),
        pltpu.make_async_copy(bias_hbm, bias_ref, load_sem.at[5]),
        pltpu.make_async_copy(tcols_hbm, tile_cols, load_sem.at[6]),
        pltpu.make_async_copy(trows_hbm, tile_rows, load_sem.at[7]),
        pltpu.make_async_copy(send_hbm, send_rows, load_sem.at[8]),
    ]
    for load in reversed(loads):
        load.start()

    barrier = pltpu.get_barrier_semaphore()
    partners = [*to_z.values(), *to_y.values(), *to_x.values(), twin]
    for partner in partners:
        pl.semaphore_signal(barrier, inc=1, device_id=partner, device_id_type=MESH)

    loads[8].wait()
    loads[0].wait()
    picked = []
    lanes = lax.broadcasted_iota(jnp.int32, (16, F_IN), 0)
    for j in range(SEND):
        row = send_rows[0, 0, j]
        group = xn[pl.ds((row >> 4) * 16, 16), pl.ds(0, F_IN)].astype(jnp.float32)
        picked.append(jnp.sum(jnp.where(lanes == (row & 15), group, 0.0), axis=0, keepdims=True))
    mine[...] = jnp.concatenate(picked, axis=0)

    pl.semaphore_wait(barrier, len(partners))

    sent = []
    for k in reversed(ring_order(nz)):
        c = copy(mine, zbuf.at[z], zs.at[k], zr.at[k], to_z[k])
        c.start()
        sent.append(c)
    zbuf[z] = mine[...]

    loads[1].wait()
    loads[7].wait()
    source = lax.broadcasted_iota(jnp.int32, (BS, BS), 0)
    target = lax.broadcasted_iota(jnp.int32, (BS, BS), 1)
    wanted = ((target % 64) // SEND) * (2 * SEND) + (target // 64) * SEND + target % SEND
    order = (source == wanted).astype(jnp.bfloat16)

    @pl.loop(0, tiles // 4)
    def _(i):
        block = vals[pl.ds(i * 4, 4)].reshape(4 * BS, BS)
        moved = jnp.dot(block, order, preferred_element_type=jnp.float32)
        vals[pl.ds(i * 4, 4)] = moved.astype(jnp.bfloat16).reshape(4, BS, BS)

    row_of = [tile_rows[0, 0, t] for t in range(tiles)]

    @pl.loop(0, tiles)
    def _(t):
        own = tile_rows[0, 0, t]
        best = jnp.int32(0)
        for s in range(tiles):
            best = jnp.maximum(best, ((row_of[s] == own) & (s < t)).astype(jnp.int32) * (s + 1))
        links[t] = best

    @pl.loop(0, rb)
    def _(r):
        best = jnp.int32(0)
        for s in range(tiles):
            best = jnp.maximum(best, (row_of[s] == r).astype(jnp.int32) * (s + 1))
        links[64 + r] = best

    prods[0] = jnp.zeros((BS, F_IN), jnp.float32)

    def place(x_, y_):
        return pl.ds(pl.multiple_of(((x_ * YLO + y_ % YLO) * nyh + y_ // YLO) * chunk, 32), chunk)

    for k in ring_order(nz):
        copy(mine, zbuf.at[wrap(z - k, nz)], zs.at[k], zr.at[k], to_z[k]).wait_recv()
    shared[core, place(x, y)] = zbuf[...].reshape(chunk, F_IN).astype(jnp.bfloat16)

    def send_x(k):
        where = shared.at[core, place(x, wrap(y - k, ny))]
        for i, step in enumerate((1, NX - 1)):
            c = copy(where, where, xs.at[i, k], xr.at[i, k], to_x[step])
            c.start()
            sent.append(c)

    def to_twin(far, k):
        where = shared.at[core, place(wrap(x - far, NX), wrap(y - k, ny))]
        c = copy(where, where, cs.at[far, k], cr.at[far, k], twin)
        c.start()
        sent.append(c)

    def from_y(k):
        where = shared.at[core, place(x, wrap(y - k, ny))]
        copy(where, where, ys.at[k], yr.at[k], to_y[k]).wait_recv()
        send_x(k)
        to_twin(0, k)

    def from_x(k):
        for i, step in enumerate((1, NX - 1)):
            where = shared.at[core, place(wrap(x - step, NX), wrap(y - k, ny))]
            copy(where, where, xs.at[i, k], xr.at[i, k], to_x[step]).wait_recv()
            if (k < ny // 2) == (i == 0):
                c = copy(where, where, rs.at[k], rr.at[k], to_x[step])
                c.start()
                sent.append(c)
            to_twin(step, k)

    send_x(0)
    own = shared.at[core, place(x, y)]
    for k in reversed(ring_order(ny)):
        c = copy(own, own, ys.at[k], yr.at[k], to_y[k])
        c.start()
        sent.append(c)
    to_twin(0, 0)
    arrivals = ring_order(ny)
    behind = [0, *arrivals]
    for n, k in enumerate(arrivals):
        from_y(k)
        if n != 1:
            from_x(behind.pop(0))
    for k in behind:
        from_x(k)
    for k in (0, *arrivals):
        where = shared.at[core, place(wrap(x + 2, NX), wrap(y - k, ny))]
        copy(where, where, rs.at[k], rr.at[k], to_x[1]).wait_recv()
        to_twin(2, k)
    for far in (0, 1, 3, 2):
        for k in (0, *arrivals):
            where = shared.at[1 - core, place(wrap(x - far, NX), wrap(y - k, ny))]
            copy(where, where, cs.at[far, k], cr.at[far, k], twin).wait_recv()

    loads[6].wait()
    for t in range(tiles):
        here = pl.ds(tile_cols[0, 0, t] * 64, 64)
        taken = jnp.concatenate([shared[0, here], shared[1, here]], axis=0)
        prods[t + 1] = jnp.dot(vals[t], taken, preferred_element_type=jnp.float32)

    @pl.loop(0, tiles)
    def _(t):
        prods[t + 1] = prods[t + 1] + prods[links[t]]

    for load in loads[2:6]:
        load.wait()
    step_rows = 2 * BS

    @pl.loop(0, rows // step_rows)
    def _(i):
        here = pl.ds(pl.multiple_of(i * step_rows, step_rows), step_rows)
        neigh = jnp.concatenate([prods[links[64 + 2 * i]], prods[links[65 + 2 * i]]], axis=0)
        xn[here, pl.ds(F_IN, F_IN)] = neigh.astype(jnp.bfloat16)
        pre = jnp.dot(xn[here], w[...], preferred_element_type=jnp.float32) + bias_ref[...]
        sig = jax.nn.sigmoid(pre)
        act[here] = (pre * sig).astype(jnp.bfloat16)
        gp[here] = (gout[here].astype(jnp.float32) * sig * (1.0 + pre * (1.0 - sig))).astype(jnp.bfloat16)

    grads = lax.dot_general(xn[...], gp[...], (((0,), (0,)), ((), ())), preferred_element_type=jnp.float32)
    for s in range(2):
        for m in range(32):
            r, l = F_IN * s + 8 * (m // 2), 128 * (m % 2)
            part[s, m] = grads[r:r + 8, l:l + 128]

    c = copy(part.at[1 - core], rx_core, r0, r1, twin)
    c.start()
    sent.append(c)
    c.wait_recv()
    half[...] = part[core] + rx_core[...]

    def hops(d):
        return min(d[0], NX - d[0]) + min(d[1], ny - d[1])

    plane = sorted(((i, j) for i in range(NX) for j in range(ny) if i or j), key=hops)

    def to_plane(d):
        return at(wrap(x + d[0], NX), wrap(y + d[1], ny), z, core)

    def tile_of(d, sign):
        return wrap(x + sign * d[0], NX) * ny + wrap(y + sign * d[1], ny)

    for d in reversed(plane):
        c = copy(half.at[tile_of(d, 1)], rx_xy.at[d[0], d[1]], rxs.at[d[0], d[1]], rxr.at[d[0], d[1]], to_plane(d))
        c.start()
        sent.append(c)
    total = half[x * ny + y]
    for d in plane:
        copy(half.at[0], rx_xy.at[d[0], d[1]], rxs.at[d[0], d[1]], rxr.at[d[0], d[1]], to_plane(d)).wait_recv()
        total = total + rx_xy[d[0], d[1]]
    tile[...] = total
    for k in reversed(ring_order(nz)):
        c = copy(tile, rx_z.at[z], rzs.at[k], rzr.at[k], to_z[k])
        c.start()
        sent.append(c)
    rx_z[z] = total
    for k in ring_order(nz):
        copy(tile, rx_z.at[wrap(z - k, nz)], rzs.at[k], rzr.at[k], to_z[k]).wait_recv()
    total = rx_z[0]
    for k in range(1, nz):
        total = total + rx_z[k]
    nodes = rows * lax.axis_size("blk") * lax.axis_size("grp")
    factor = 1.0 / jnp.sqrt(jnp.float32(nodes))
    final[core, x * ny + y] = total * factor
    own = final.at[core, x * ny + y]
    for d in reversed(plane):
        c = copy(own, own, fxs.at[d[0], d[1]], fxr.at[d[0], d[1]], to_plane(d))
        c.start()
        sent.append(c)
    for d in ((0, 0), *plane):
        where = final.at[core, tile_of(d, -1)]
        if d != (0, 0):
            copy(where, where, fxs.at[d[0], d[1]], fxr.at[d[0], d[1]], to_plane(d)).wait_recv()
        c = copy(where, where, fcs.at[d[0], d[1]], fcr.at[d[0], d[1]], twin)
        c.start()
        sent.append(c)
    for d in ((0, 0), *plane):
        where = final.at[1 - core, tile_of(d, -1)]
        copy(where, where, fcs.at[d[0], d[1]], fcr.at[d[0], d[1]], twin).wait_recv()
    for s, ref in enumerate((gs_ref, gn_ref)):
        for m in range(32):
            ref[8 * (m // 2):8 * (m // 2) + 8, 128 * (m % 2):128 * (m % 2) + 128] = final[s, m]
    for c in sent:
        c.wait_send()


def shards(mesh_shape, features, send_rows, tile_rows, tile_cols, tile_vals, w_self, w_neigh, bias, grad_out):
    rows = features.shape[0]
    tiles = tile_vals.shape[2]
    nx_ylo, rest = mesh_shape
    nyh = 4
    nz = rest // (2 * nyh)
    ny = nyh * YLO
    ndev = nx_ylo * rest
    bf16, f32 = jnp.bfloat16, jnp.float32
    dma = pltpu.SemaphoreType.DMA
    hbm = pl.BlockSpec(memory_space=pltpu.HBM)
    vmem = pl.BlockSpec(memory_space=pltpu.VMEM)
    return pl.pallas_call(
        functools.partial(kernel, (rows, tiles, nz, ny)),
        out_shape=(
            jax.ShapeDtypeStruct((rows, HID), bf16),
            jax.ShapeDtypeStruct((F_IN, HID), f32),
            jax.ShapeDtypeStruct((F_IN, HID), f32),
        ),
        in_specs=[hbm] * 9,
        out_specs=(vmem, vmem, vmem),
        scratch_shapes=[
            pltpu.SMEM((1, 1, SEND), jnp.int32),
            pltpu.SMEM((1, 1, tiles), jnp.int32),
            pltpu.SMEM((1, 1, tiles), jnp.int32),
            pltpu.VMEM((1, HID), f32),
            pltpu.VMEM((rows, 2 * F_IN), bf16),
            pltpu.VMEM((2 * F_IN, HID), bf16),
            pltpu.VMEM((tiles, BS, BS), bf16),
            pltpu.VMEM((rows, HID), bf16),
            pltpu.VMEM((rows, HID), bf16),
            pltpu.VMEM((nz, SEND, F_IN), f32),
            pltpu.VMEM((SEND, F_IN), f32),
            pltpu.VMEM((2, ndev // 2 * SEND, F_IN), bf16),
            pltpu.VMEM((tiles + 1, BS, F_IN), f32),
            pltpu.SMEM((128,), jnp.int32),
            pltpu.VMEM((2, 32, 8, 128), f32),
            pltpu.VMEM((32, 8, 128), f32),
            pltpu.VMEM((32, 8, 128), f32),
            pltpu.VMEM((NX, ny, 8, 128), f32),
            pltpu.VMEM((8, 128), f32),
            pltpu.VMEM((nz, 8, 128), f32),
            pltpu.VMEM((2, 32, 8, 128), f32),
            dma((9,)),
            dma((nz,)), dma((nz,)), dma((ny,)), dma((ny,)), dma((2, ny)), dma((2, ny)),
            dma((ny,)), dma((ny,)), dma((NX, ny)), dma((NX, ny)),
            dma, dma, dma((NX, ny)), dma((NX, ny)), dma((nz,)), dma((nz,)),
            dma((NX, ny)), dma((NX, ny)), dma((NX, ny)), dma((NX, ny)),
        ],
        compiler_params=pltpu.CompilerParams(
            collective_id=0, has_side_effects=True, vmem_limit_bytes=40 * 1024 * 1024
        ),
    )(*(
        pltpu.with_memory_space_constraint(a, pltpu.HBM)
        for a in (send_rows, tile_rows, tile_cols, features, tile_vals, w_self, w_neigh, bias.reshape(1, HID), grad_out)
    ))


def solution(mesh):
    in_specs = (
        P(("blk", "grp"), None),
        P("blk", "grp", None),
        P("blk", "grp", None),
        P("blk", "grp", None),
        P("blk", "grp", None, None, None),
        P(),
        P(),
        P(),
        P(("blk", "grp"), None),
    )
    out_specs = (P(("blk", "grp"), None), P(), P())
    body = functools.partial(shards, (mesh.shape["blk"], mesh.shape["grp"]))
    return jax.shard_map(body, mesh=mesh, in_specs=in_specs, out_specs=out_specs, check_vma=False)
```

time: 88.6 us -> 75 us (0.85)
  local copies, waits for them, and re-layouts: 9.43 us -> 2.28 us
  Pallas kernels: 78.2 us -> 71.9 us
    unnamed x21 -> x3, local copies, waits for them, and re-layouts: 9.43 us -> 2.28 us
    pallas_call x1, Pallas kernels: 78.2 us -> 71.9 us  [shards(): pl.pallas_call(functools.partial(kernel, (rows, tiles, nz, ny)), out_shap...]
where the time goes in v2:
time: 75 us; the launch traced here: 74.8 us
  Pallas kernels  71.9 us (96%)
  local copies, waits for them, and re-layouts  2.28 us (3%)
    pallas_call x1, Pallas kernels, shards(): pl.pallas_call(functools.partial(kernel, (rows, tiles, nz, ny)), out_shap...  71.9 us
    unnamed x3, local copies, waits for them, and re-layouts  2.28 us

profile of v2, /device:TPU:1, one launch (start us, length us, event | category | flops | bytes accessed | tf_op | source)
XLA Modules:
  0.0 74.8 jit_solution(16600293152978833348)
XLA Ops:
  0.6 71.9 %shard_map.112 = (bf16[2048,256]{1,0:T(8,128)(2,1)S(1)}, f32[128,256]{1,0:T(8,128)S(1)}, f32[128,256]{1,0:T(8,128)S(1)}) custom-call(s32[1,1,8]{2,1,0:T(1,128)} %send_hbm.1, s32[1,1,32]{2,1,0:T(1,128)} %trows_hbm.1, s32[1,1,32]{2,1,0:T(1,128)} %tcols_hbm.1, bf16[2048,128]{1,0:T(8,128)(2,1)} %feat_hbm.1, bf16[1,1,32,128,128]{4,3,2,1,0:T(8,128)(2,1)} %vals_hbm.1, ...), custom_call_target="tpu_custom_call" | custom-call | tf_op jit(solution)/shard_map/pallas_call | solution.py:293
  72.5 1.0 %copy.15 = bf16[2048,256]{1,0:T(8,128)(2,1)} copy(bf16[2048,256]{1,0:T(8,128)(2,1)S(1)} %get-tuple-element.6) | data formatting | bytes 2097152
  73.5 0.7 copy.16
  74.2 0.7 copy.17

commit v3 on v2

v3 whole, which is shorter than its diff:
```python
import functools

import jax
import jax.numpy as jnp
from jax import lax
from jax.experimental import pallas as pl
from jax.experimental.pallas import tpu as pltpu
from jax.sharding import PartitionSpec as P

MESH = pl.DeviceIdType.MESH
BS = 128
F_IN = 128
HID = 256
SEND = 8
NX = 4
YLO = 2


def ring_order(n):
    return sorted(range(1, n), key=lambda k: (min(k, n - k), k))


def kernel(
    dims,
    send_hbm, trows_hbm, tcols_hbm,
    feat_hbm, vals_hbm, ws_hbm, wn_hbm, bias_hbm, gout_hbm,
    act, gs_ref, gn_ref,
    send_rows, tile_rows, tile_cols, bias_ref, xn, w, vals, gout, gp, zbuf, mine, shared, prods, links,
    part, rx_core, half, rx_xy, tile, rx_z, final,
    load_sem, zs, zr, ys, yr, xs, xr, rs, rr, cs, cr, ps, pr, fs, fr,
):
    rows, tiles, nz, ny = dims
    nyh = ny // YLO
    rb = rows // BS
    chunk = nz * SEND
    blk, grp = lax.axis_index("blk"), lax.axis_index("grp")
    core = grp & 1
    yhi = lax.div(grp, 2 * nz)
    z = (grp >> 1) - yhi * nz
    y = yhi * YLO + (blk & 1)
    x = blk >> 1

    xk = [(x + k) & (NX - 1) for k in range(NX)]
    yk = [(y + k) & (ny - 1) for k in range(ny)]
    zk = [z] + [jnp.where(z + k >= nz, z + k - nz, z + k) for k in range(1, nz)]
    y_grp = [(v >> 1) * (2 * nz) for v in yk]
    y_row = [((v & 1) * nyh + (v >> 1)) * chunk for v in yk]
    x_row = [v * (ny * chunk) for v in xk]
    z_core = 2 * z + core

    def on(i, j):
        return {"blk": xk[i] * YLO + (yk[j] & 1), "grp": y_grp[j] + z_core}

    def copy(src, dst, send, recv, to):
        return pltpu.make_async_remote_copy(
            src_ref=src, dst_ref=dst, send_sem=send, recv_sem=recv, device_id=to, device_id_type=MESH
        )

    to_z = {k: {"blk": blk, "grp": y_grp[0] + 2 * zk[k] + core} for k in range(1, nz)}
    to_y = {k: on(0, k) for k in range(1, ny)}
    to_x = {k: on(k, 0) for k in (1, NX - 1)}
    twin = {"blk": blk, "grp": grp + 1 - 2 * core}

    barrier = pltpu.get_barrier_semaphore()
    partners = [*to_z.values(), *to_y.values(), *to_x.values(), twin]
    for partner in partners:
        pl.semaphore_signal(barrier, inc=1, device_id=partner, device_id_type=MESH)

    loads = [
        pltpu.make_async_copy(send_hbm, send_rows, load_sem.at[8]),
        pltpu.make_async_copy(feat_hbm, xn.at[:, pl.ds(0, F_IN)], load_sem.at[0]),
        pltpu.make_async_copy(trows_hbm, tile_rows, load_sem.at[7]),
        pltpu.make_async_copy(vals_hbm.at[0, 0], vals, load_sem.at[1]),
        pltpu.make_async_copy(tcols_hbm, tile_cols, load_sem.at[6]),
        pltpu.make_async_copy(ws_hbm, w.at[pl.ds(0, F_IN)], load_sem.at[3]),
        pltpu.make_async_copy(wn_hbm, w.at[pl.ds(F_IN, F_IN)], load_sem.at[4]),
        pltpu.make_async_copy(bias_hbm, bias_ref, load_sem.at[5]),
        pltpu.make_async_copy(gout_hbm, gout, load_sem.at[2]),
    ]
    for load in loads:
        load.start()
    loads[0].wait()
    loads[1].wait()
    picked = []
    lanes = lax.broadcasted_iota(jnp.int32, (16, F_IN), 0)
    for j in range(SEND):
        row = send_rows[0, 0, j]
        group = xn[pl.ds((row >> 4) * 16, 16), pl.ds(0, F_IN)].astype(jnp.float32)
        picked.append(jnp.sum(jnp.where(lanes == (row & 15), group, 0.0), axis=0, keepdims=True))
    mine[...] = jnp.concatenate(picked, axis=0)

    pl.semaphore_wait(barrier, len(partners))

    for k in reversed(ring_order(nz)):
        copy(mine, zbuf.at[z], zs, zr, to_z[k]).start()
    zbuf[z] = mine[...]

    loads[2].wait()
    loads[3].wait()
    source = lax.broadcasted_iota(jnp.int32, (BS, BS), 0)
    target = lax.broadcasted_iota(jnp.int32, (BS, BS), 1)
    wanted = ((target % 64) // SEND) * (2 * SEND) + (target // 64) * SEND + target % SEND
    order = (source == wanted).astype(jnp.bfloat16)

    @pl.loop(0, tiles // 4)
    def _(i):
        block = vals[pl.ds(i * 4, 4)].reshape(4 * BS, BS)
        moved = jnp.dot(block, order, preferred_element_type=jnp.float32)
        vals[pl.ds(i * 4, 4)] = moved.astype(jnp.bfloat16).reshape(4, BS, BS)

    row_of = [tile_rows[0, 0, t] for t in range(tiles)]

    @pl.loop(0, tiles)
    def _(t):
        own = tile_rows[0, 0, t]
        best = jnp.int32(0)
        for s in range(tiles):
            best = jnp.maximum(best, ((row_of[s] == own) & (s < t)).astype(jnp.int32) * (s + 1))
        links[t] = best

    @pl.loop(0, rb)
    def _(r):
        best = jnp.int32(0)
        for s in range(tiles):
            best = jnp.maximum(best, (row_of[s] == r).astype(jnp.int32) * (s + 1))
        links[64 + r] = best

    prods[0] = jnp.zeros((BS, F_IN), jnp.float32)

    def place(i, j):
        return shared.at[core, pl.ds(pl.multiple_of(x_row[i] + y_row[j], 32), chunk)]

    def slab(core_, i):
        return shared.at[core_, pl.ds(pl.multiple_of(x_row[i], 32), ny * chunk)]

    others = zbuf.at[pl.ds(0, nz - 1)]
    copy(others, others, zs, zr, twin).wait()
    own = place(0, 0)
    own[...] = zbuf[...].reshape(chunk, F_IN).astype(jnp.bfloat16)

    ends = ((1, NX - 1), (NX - 1, 1))

    def send_x(k):
        where = place(0, -k)
        for i, (step, _) in enumerate(ends):
            copy(where, where, xs, xr.at[i, k], to_x[step]).start()

    def from_y(k):
        where = place(0, -k)
        copy(where, where, ys, yr.at[k], to_y[k]).wait_recv()
        send_x(k)

    def from_x(k):
        for i, (step, origin) in enumerate(ends):
            where = place(origin, -k)
            copy(where, where, xs, xr.at[i, k], to_x[step]).wait_recv()
            if (k < ny // 2) == (i == 0):
                copy(where, where, rs, rr, to_x[step]).start()

    def to_twin(i):
        where = slab(core, i)
        copy(where, where, cs, cr.at[i], twin).start()

    send_x(0)
    for k in reversed(ring_order(ny)):
        copy(own, own, ys, yr.at[k], to_y[k]).start()
    arrivals = ring_order(ny)
    behind = [0, *arrivals]
    for n, k in enumerate(arrivals):
        from_y(k)
        if n != 1:
            from_x(behind.pop(0))
    to_twin(0)
    for k in behind:
        from_x(k)
    to_twin(1)
    to_twin(NX - 1)
    where = slab(core, 2)
    copy(where, where, rs, rr, twin).wait_recv()
    to_twin(2)
    loads[4].wait()
    for load in loads[5:]:
        load.wait()
    seven = shared.at[0, pl.ds(0, (ny - 1) * chunk)]
    copy(seven, seven, ys, yr.at[1], twin).wait_send()
    for _ in range(2):
        copy(where, where, xs, xr.at[0, 0], twin).wait_send()
    copy(where, where, rs, rr, twin).wait_send()
    for i in (0, 1, NX - 1, 2):
        where = slab(1 - core, i)
        copy(where, where, cs, cr.at[i], twin).wait()

    for t in range(tiles):
        here = pl.ds(tile_cols[0, 0, t] * 64, 64)
        taken = jnp.concatenate([shared[0, here], shared[1, here]], axis=0)
        prods[t + 1] = jnp.dot(vals[t], taken, preferred_element_type=jnp.float32)

    @pl.loop(0, tiles)
    def _(t):
        prods[t + 1] = prods[t + 1] + prods[links[t]]

    step_rows = 2 * BS

    @pl.loop(0, rows // step_rows)
    def _(i):
        here = pl.ds(pl.multiple_of(i * step_rows, step_rows), step_rows)
        neigh = jnp.concatenate([prods[links[64 + 2 * i]], prods[links[65 + 2 * i]]], axis=0)
        xn[here, pl.ds(F_IN, F_IN)] = neigh.astype(jnp.bfloat16)
        pre = jnp.dot(xn[here], w[...], preferred_element_type=jnp.float32) + bias_ref[...]
        sig = jax.nn.sigmoid(pre)
        act[here] = (pre * sig).astype(jnp.bfloat16)
        gp[here] = (gout[here].astype(jnp.float32) * sig * (1.0 + pre * (1.0 - sig))).astype(jnp.bfloat16)

    grads = lax.dot_general(xn[...], gp[...], (((0,), (0,)), ((), ())), preferred_element_type=jnp.float32)
    for s in range(2):
        for m in range(32):
            r, l = F_IN * s + 8 * (m // 2), 128 * (m % 2)
            part[s, m] = grads[r:r + 8, l:l + 128]

    c = copy(part.at[1 - core], rx_core, ps.at[0], pr.at[0], twin)
    c.start()
    c.wait_recv()
    half[...] = part[core] + rx_core[...]
    plane = [(i, j) for i in range(NX) for j in range(ny) if i or j]
    plane.sort(key=lambda d: -min(d[0], NX - d[0]) - min(d[1], ny - d[1]))
    x_tile = [v * ny for v in xk]
    for i, j in plane:
        copy(half.at[x_tile[i] + yk[j]], rx_xy.at[i * ny + j - 1], ps.at[1], pr.at[1], on(i, j)).start()
    c.wait_send()
    count = NX * ny - 1
    most = rx_xy.at[pl.ds(0, count)]
    copy(most, most, ps.at[1], pr.at[1], twin).wait()
    total = half[x_tile[0] + y]
    for n in range(count):
        total = total + rx_xy[n]
    tile[...] = total
    for k in reversed(ring_order(nz)):
        copy(tile, rx_z.at[z], ps.at[2], pr.at[2], to_z[k]).start()
    rx_z[z] = total
    others = rx_z.at[pl.ds(0, nz - 1)]
    copy(others, others, ps.at[2], pr.at[2], twin).wait()
    total = rx_z[0]
    for k in range(1, nz):
        total = total + rx_z[k]
    nodes = rows * lax.axis_size("blk") * lax.axis_size("grp")
    factor = 1.0 / jnp.sqrt(jnp.float32(nodes))
    own = final.at[core, x_tile[0] + y]
    own[...] = total * factor
    for i, j in plane:
        copy(own, own, fs.at[0], fr.at[0], on(i, j)).start()
    most = final.at[0, pl.ds(0, count)]
    copy(most, most, fs.at[0], fr.at[0], twin).wait()
    c = copy(final.at[core], final.at[core], fs.at[1], fr.at[1], twin)
    c.start()
    c.wait_send()
    copy(final.at[1 - core], final.at[1 - core], fs.at[1], fr.at[1], twin).wait_recv()
    for s, ref in enumerate((gs_ref, gn_ref)):
        for m in range(32):
            ref[8 * (m // 2):8 * (m // 2) + 8, 128 * (m % 2):128 * (m % 2) + 128] = final[s, m]


def store(act, gs, gn, act_out, gs_out, gn_out, sem):
    copies = [
        pltpu.make_async_copy(src, dst, sem.at[i])
        for i, (src, dst) in enumerate(((act, act_out), (gs, gs_out), (gn, gn_out)))
    ]
    for c in copies:
        c.start()
    for c in copies:
        c.wait()


def shards(mesh_shape, features, send_rows, tile_rows, tile_cols, tile_vals, w_self, w_neigh, bias, grad_out):
    rows = features.shape[0]
    tiles = tile_vals.shape[2]
    nx_ylo, rest = mesh_shape
    nyh = 4
    nz = rest // (2 * nyh)
    ny = nyh * YLO
    ndev = nx_ylo * rest
    bf16, f32 = jnp.bfloat16, jnp.float32
    dma = pltpu.SemaphoreType.DMA
    hbm = pl.BlockSpec(memory_space=pltpu.HBM)
    vmem = pl.BlockSpec(memory_space=pltpu.VMEM)
    outs = (
        jax.ShapeDtypeStruct((rows, HID), bf16),
        jax.ShapeDtypeStruct((F_IN, HID), f32),
        jax.ShapeDtypeStruct((F_IN, HID), f32),
    )
    results = pl.pallas_call(
        functools.partial(kernel, (rows, tiles, nz, ny)),
        out_shape=outs,
        in_specs=[hbm] * 9,
        out_specs=(vmem, vmem, vmem),
        scratch_shapes=[
            pltpu.SMEM((1, 1, SEND), jnp.int32),
            pltpu.SMEM((1, 1, tiles), jnp.int32),
            pltpu.SMEM((1, 1, tiles), jnp.int32),
            pltpu.VMEM((1, HID), f32),
            pltpu.VMEM((rows, 2 * F_IN), bf16),
            pltpu.VMEM((2 * F_IN, HID), bf16),
            pltpu.VMEM((tiles, BS, BS), bf16),
            pltpu.VMEM((rows, HID), bf16),
            pltpu.VMEM((rows, HID), bf16),
            pltpu.VMEM((nz, SEND, F_IN), f32),
            pltpu.VMEM((SEND, F_IN), f32),
            pltpu.VMEM((2, ndev // 2 * SEND, F_IN), bf16),
            pltpu.VMEM((tiles + 1, BS, F_IN), f32),
            pltpu.SMEM((128,), jnp.int32),
            pltpu.VMEM((2, 32, 8, 128), f32),
            pltpu.VMEM((32, 8, 128), f32),
            pltpu.VMEM((32, 8, 128), f32),
            pltpu.VMEM((NX * ny, 8, 128), f32),
            pltpu.VMEM((8, 128), f32),
            pltpu.VMEM((nz, 8, 128), f32),
            pltpu.VMEM((2, 32, 8, 128), f32),
            dma((9,)), dma, dma, dma, dma((ny,)), dma, dma((2, ny)), dma, dma, dma, dma((NX,)),
            dma((3,)), dma((3,)), dma((2,)), dma((2,)),
        ],
        compiler_params=pltpu.CompilerParams(
            collective_id=0, has_side_effects=True, vmem_limit_bytes=40 * 1024 * 1024
        ),
    )(*(
        pltpu.with_memory_space_constraint(a, pltpu.HBM)
        for a in (send_rows, tile_rows, tile_cols, features, tile_vals, w_self, w_neigh, bias.reshape(1, HID), grad_out)
    ))
    anywhere = pl.BlockSpec(memory_space=pl.ANY)
    return pl.pallas_call(
        store,
        out_shape=outs,
        in_specs=[anywhere] * 3,
        out_specs=(anywhere,) * 3,
        scratch_shapes=[dma((3,))],
    )(*results)


def solution(mesh):
    in_specs = (
        P(("blk", "grp"), None),
        P("blk", "grp", None),
        P("blk", "grp", None),
        P("blk", "grp", None),
        P("blk", "grp", None, None, None),
        P(),
        P(),
        P(),
        P(("blk", "grp"), None),
    )
    out_specs = (P(("blk", "grp"), None), P(), P())
    body = functools.partial(shards, (mesh.shape["blk"], mesh.shape["grp"]))
    return jax.shard_map(body, mesh=mesh, in_specs=in_specs, out_specs=out_specs, check_vma=False)
```

time: 75 us -> 114 us (1.52)
  Pallas kernels: 71.9 us -> 111 us
    pallas_call x0 -> x1, Pallas kernels: none -> 40.8 us  [shards(): pl.pallas_call(store, out_shape=outs, in_specs=[anywhere] * 3, out_specs=...]
    pallas_call x1, Pallas kernels: 71.9 us -> 69.8 us  [shards(): pl.pallas_call(functools.partial(kernel, (rows, tiles, nz, ny)), out_shap...]
    unnamed x3 -> x6, local copies, waits for them, and re-layouts: 2.28 us -> 2.24 us
where the time goes in v3:
time: 114 us; the launch traced here: 113 us
  Pallas kernels  111 us (97%)
  local copies, waits for them, and re-layouts  2.24 us (2%)
    pallas_call x1, Pallas kernels, shards(): pl.pallas_call(functools.partial(kernel, (rows, tiles, nz, ny)), out_shap...  69.8 us
    pallas_call x1, Pallas kernels, shards(): pl.pallas_call(store, out_shape=outs, in_specs=[anywhere] * 3, out_specs=...  40.8 us

profile of v3, /device:TPU:1, one launch (start us, length us, event | category | flops | bytes accessed | tf_op | source)
XLA Modules:
  0.0 113.5 jit_solution(8115692235688045873)
XLA Ops:
  0.6 69.8 %shard_map.112 = (bf16[2048,256]{1,0:T(8,128)(2,1)S(1)}, f32[128,256]{1,0:T(8,128)S(1)}, f32[128,256]{1,0:T(8,128)S(1)}) custom-call(s32[1,1,8]{2,1,0:T(1,128)} %send_hbm.1, s32[1,1,32]{2,1,0:T(1,128)} %trows_hbm.1, s32[1,1,32]{2,1,0:T(1,128)} %tcols_hbm.1, bf16[2048,128]{1,0:T(8,128)(2,1)} %feat_hbm.1, bf16[1,1,32,128,128]{4,3,2,1,0:T(8,128)(2,1)} %vals_hbm.1, ...), custom_call_target="tpu_custom_call" | custom-call | tf_op jit(solution)/shard_map/pallas_call | solution.py:290
  70.4 0.0 copy-start
  70.4 1.0 copy-done
  71.4 0.0 copy-start.1
  71.4 0.6 copy-done.1
  72.0 0.0 copy-start.2
  72.0 0.6 copy-done.2
  72.6 40.8 %shard_map.113 = (bf16[2048,256]{1,0:T(8,128)(2,1)}, f32[128,256]{1,0:T(8,128)}, f32[128,256]{1,0:T(8,128)}) custom-call(bf16[2048,256]{1,0:T(8,128)(2,1)} %copy-done, f32[128,256]{1,0:T(8,128)} %copy-done.1, f32[128,256]{1,0:T(8,128)} %copy-done.2), custom_call_target="tpu_custom_call" | custom-call | tf_op jit(solution)/shard_map/pallas_call | solution.py:328
Async XLA Ops:
  70.4 1.0 copy-start
  71.4 0.6 copy-start.1
  72.0 0.6 copy-start.2

commit v4 on v3

--- a/solution.py
+++ b/solution.py
@@ -27,7 +27,7 @@
     act, gs_ref, gn_ref,
     send_rows, tile_rows, tile_cols, bias_ref, xn, w, vals, gout, gp, zbuf, mine, shared, prods, links,
     part, rx_core, half, rx_xy, tile, rx_z, final,
-    load_sem, zs, zr, ys, yr, xs, xr, rs, rr, cs, cr, ps, pr, fs, fr,
+    load_sem, zs, zr, ys, yr, xs, xr, vs, vr, cs, cr, ps, pr, fs, fr,
 ):
     rows, tiles, nz, ny = dims
     nyh = ny // YLO
@@ -58,7 +58,7 @@
 
     to_z = {k: {"blk": blk, "grp": y_grp[0] + 2 * zk[k] + core} for k in range(1, nz)}
     to_y = {k: on(0, k) for k in range(1, ny)}
-    to_x = {k: on(k, 0) for k in (1, NX - 1)}
+    to_x = {k: on(k, 0) for k in range(1, NX)}
     twin = {"blk": blk, "grp": grp + 1 - 2 * core}
 
     barrier = pltpu.get_barrier_semaphore()
@@ -138,57 +138,62 @@
     own = place(0, 0)
     own[...] = zbuf[...].reshape(chunk, F_IN).astype(jnp.bfloat16)
 
-    ends = ((1, NX - 1), (NX - 1, 1))
-
-    def send_x(k):
+    far_y, near_y, all_x = (2, ny - 2, 4, 3, ny - 3), (1, ny - 1), (2, 1, NX - 1)
+
+    def send(where, sems, to):
+        copy(where, where, *sems, to).start()
+
+    def arrived(where, recv):
+        copy(where, where, cs, recv, twin).wait_recv()
+
+    for i in all_x:
+        send(own, (xs, xr.at[i, 0]), to_x[i])
+    for k in (*far_y, *near_y):
+        send(own, (ys, yr.at[k]), to_y[k])
+    for i in reversed(all_x):
+        where = place(-i, 0)
+        arrived(where, xr.at[i, 0])
+        for n, k in enumerate(near_y):
+            send(where, (vs, vr.at[n, i]), to_y[k])
+        send(where, (cs, cr.at[i]), twin)
+    for k in far_y:
         where = place(0, -k)
-        for i, (step, _) in enumerate(ends):
-            copy(where, where, xs, xr.at[i, k], to_x[step]).start()
-
-    def from_y(k):
-        where = place(0, -k)
-        copy(where, where, ys, yr.at[k], to_y[k]).wait_recv()
-        send_x(k)
+        arrived(where, yr.at[k])
+        for i in all_x:
+            send(where, (xs, xr.at[i, k]), to_x[i])
+    for k in near_y:
+        arrived(place(0, -k), yr.at[k])
+    send(slab(core, 0), (cs, cr.at[0]), twin)
 
     def from_x(k):
-        for i, (step, origin) in enumerate(ends):
-            where = place(origin, -k)
-            copy(where, where, xs, xr.at[i, k], to_x[step]).wait_recv()
-            if (k < ny // 2) == (i == 0):
-                copy(where, where, rs, rr, to_x[step]).start()
-
-    def to_twin(i):
-        where = slab(core, i)
-        copy(where, where, cs, cr.at[i], twin).start()
-
-    send_x(0)
-    for k in reversed(ring_order(ny)):
-        copy(own, own, ys, yr.at[k], to_y[k]).start()
-    arrivals = ring_order(ny)
-    behind = [0, *arrivals]
-    for n, k in enumerate(arrivals):
-        from_y(k)
-        if n != 1:
-            from_x(behind.pop(0))
-    to_twin(0)
-    for k in behind:
+        for i in reversed(all_x):
+            where = place(-i, -k)
+            arrived(where, xr.at[i, k])
+            send(where, (cs, cr.at[i]), twin)
+
+    for k in far_y[:2]:
         from_x(k)
-    to_twin(1)
-    to_twin(NX - 1)
-    where = slab(core, 2)
-    copy(where, where, rs, rr, twin).wait_recv()
-    to_twin(2)
+    for i in reversed(all_x):
+        for n, k in enumerate(near_y):
+            where = place(-i, -k)
+            arrived(where, vr.at[n, i])
+            send(where, (cs, cr.at[i]), twin)
+    for k in far_y[2:]:
+        from_x(k)
     loads[4].wait()
     for load in loads[5:]:
         load.wait()
-    seven = shared.at[0, pl.ds(0, (ny - 1) * chunk)]
-    copy(seven, seven, ys, yr.at[1], twin).wait_send()
-    for _ in range(2):
-        copy(where, where, xs, xr.at[0, 0], twin).wait_send()
-    copy(where, where, rs, rr, twin).wait_send()
-    for i in (0, 1, NX - 1, 2):
-        where = slab(1 - core, i)
-        copy(where, where, cs, cr.at[i], twin).wait()
+
+    def all_sent(sem, chunks):
+        where = shared.at[0, pl.ds(0, chunks * chunk)]
+        copy(where, where, sem, cr.at[0], twin).wait_send()
+
+    all_sent(ys, ny - 1)
+    all_sent(xs, 3 * 6)
+    all_sent(vs, 3 * 2)
+    all_sent(cs, 4 * ny)
+    for i in range(NX):
+        arrived(slab(1 - core, -i), cr.at[i])
 
     for t in range(tiles):
         here = pl.ds(tile_cols[0, 0, t] * 64, 64)
@@ -259,17 +264,6 @@
             ref[8 * (m // 2):8 * (m // 2) + 8, 128 * (m % 2):128 * (m % 2) + 128] = final[s, m]
 
 
-def store(act, gs, gn, act_out, gs_out, gn_out, sem):
-    copies = [
-        pltpu.make_async_copy(src, dst, sem.at[i])
-        for i, (src, dst) in enumerate(((act, act_out), (gs, gs_out), (gn, gn_out)))
-    ]
-    for c in copies:
-        c.start()
-    for c in copies:
-        c.wait()
-
-
 def shards(mesh_shape, features, send_rows, tile_rows, tile_cols, tile_vals, w_self, w_neigh, bias, grad_out):
     rows = features.shape[0]
     tiles = tile_vals.shape[2]
@@ -287,7 +281,7 @@
         jax.ShapeDtypeStruct((F_IN, HID), f32),
         jax.ShapeDtypeStruct((F_IN, HID), f32),
     )
-    results = pl.pallas_call(
+    return pl.pallas_call(
         functools.partial(kernel, (rows, tiles, nz, ny)),
         out_shape=outs,
         in_specs=[hbm] * 9,
@@ -314,7 +308,7 @@
             pltpu.VMEM((8, 128), f32),
             pltpu.VMEM((nz, 8, 128), f32),
             pltpu.VMEM((2, 32, 8, 128), f32),
-            dma((9,)), dma, dma, dma, dma((ny,)), dma, dma((2, ny)), dma, dma, dma, dma((NX,)),
+            dma((9,)), dma, dma, dma, dma((ny,)), dma, dma((NX, ny)), dma, dma((2, NX)), dma, dma((NX,)),
             dma((3,)), dma((3,)), dma((2,)), dma((2,)),
         ],
         compiler_params=pltpu.CompilerParams(
@@ -324,14 +318,6 @@
         pltpu.with_memory_space_constraint(a, pltpu.HBM)
         for a in (send_rows, tile_rows, tile_cols, features, tile_vals, w_self, w_neigh, bias.reshape(1, HID), grad_out)
     ))
-    anywhere = pl.BlockSpec(memory_space=pl.ANY)
-    return pl.pallas_call(
-        store,
-        out_shape=outs,
-        in_specs=[anywhere] * 3,
-        out_specs=(anywhere,) * 3,
-        scratch_shapes=[dma((3,))],
-    )(*results)
 
 
 def solution(mesh):

time: 114 us -> 66 us (0.58)
  Pallas kernels: 111 us -> 62.9 us
    pallas_call x1 -> x0, Pallas kernels: 40.8 us -> none  [shards(): pl.pallas_call(store, out_shape=outs, in_specs=[anywhere] * 3, out_specs=...]
    pallas_call x1, Pallas kernels: 69.8 us -> 62.9 us  [shards(): pl.pallas_call(functools.partial(kernel, (rows, tiles, nz, ny)), out_shap...]
    unnamed x6 -> x3, local copies, waits for them, and re-layouts: 2.24 us -> 2.28 us
where the time goes in v4:
time: 66 us; the launch traced here: 65.8 us
  Pallas kernels  62.9 us (95%)
  local copies, waits for them, and re-layouts  2.28 us (3%)
    pallas_call x1, Pallas kernels, shards(): pl.pallas_call(functools.partial(kernel, (rows, tiles, nz, ny)), out_shap...  62.9 us
    unnamed x3, local copies, waits for them, and re-layouts  2.28 us

profile of v4, /device:TPU:1, one launch (start us, length us, event | category | flops | bytes accessed | tf_op | source)
XLA Modules:
  0.0 65.8 jit_solution(2290162437749815425)
XLA Ops:
  0.6 62.9 %shard_map.112 = (bf16[2048,256]{1,0:T(8,128)(2,1)S(1)}, f32[128,256]{1,0:T(8,128)S(1)}, f32[128,256]{1,0:T(8,128)S(1)}) custom-call(s32[1,1,8]{2,1,0:T(1,128)} %send_hbm.1, s32[1,1,32]{2,1,0:T(1,128)} %trows_hbm.1, s32[1,1,32]{2,1,0:T(1,128)} %tcols_hbm.1, bf16[2048,128]{1,0:T(8,128)(2,1)} %feat_hbm.1, bf16[1,1,32,128,128]{4,3,2,1,0:T(8,128)(2,1)} %vals_hbm.1, ...), custom_call_target="tpu_custom_call" | custom-call | tf_op jit(solution)/shard_map/pallas_call | solution.py:284
  63.5 1.0 %copy.15 = bf16[2048,256]{1,0:T(8,128)(2,1)} copy(bf16[2048,256]{1,0:T(8,128)(2,1)S(1)} %get-tuple-element.6) | data formatting | bytes 2097152
  64.5 0.7 copy.16
  65.2 0.7 copy.17

commit v5 on v4

--- a/solution.py
+++ b/solution.py
@@ -25,7 +25,7 @@
     send_hbm, trows_hbm, tcols_hbm,
     feat_hbm, vals_hbm, ws_hbm, wn_hbm, bias_hbm, gout_hbm,
     act, gs_ref, gn_ref,
-    send_rows, tile_rows, tile_cols, bias_ref, xn, w, vals, gout, gp, zbuf, mine, shared, prods, links,
+    send_rows, tile_rows, tile_cols, bias_ref, xn, w, vals, gout, zbuf, mine, shared, prods, links,
     part, rx_core, half, rx_xy, tile, rx_z, final,
     load_sem, zs, zr, ys, yr, xs, xr, vs, vr, cs, cr, ps, pr, fs, fr,
 ):
@@ -62,7 +62,7 @@
     twin = {"blk": blk, "grp": grp + 1 - 2 * core}
 
     barrier = pltpu.get_barrier_semaphore()
-    partners = [*to_z.values(), *to_y.values(), *to_x.values(), twin]
+    partners = [*(to_z[k] for k in reversed(ring_order(nz))), *to_y.values(), *to_x.values(), twin]
     for partner in partners:
         pl.semaphore_signal(barrier, inc=1, device_id=partner, device_id_type=MESH)
 
@@ -204,19 +204,17 @@
     def _(t):
         prods[t + 1] = prods[t + 1] + prods[links[t]]
 
-    step_rows = 2 * BS
-
-    @pl.loop(0, rows // step_rows)
-    def _(i):
-        here = pl.ds(pl.multiple_of(i * step_rows, step_rows), step_rows)
-        neigh = jnp.concatenate([prods[links[64 + 2 * i]], prods[links[65 + 2 * i]]], axis=0)
-        xn[here, pl.ds(F_IN, F_IN)] = neigh.astype(jnp.bfloat16)
+    step_rows = 4 * BS
+    grads = jnp.zeros((2 * F_IN, HID), jnp.float32)
+    for i in range(rows // step_rows):
+        here = slice(i * step_rows, (i + 1) * step_rows)
+        neigh = jnp.concatenate([prods[links[64 + 4 * i + j]] for j in range(4)], axis=0)
+        xn[here, F_IN:] = neigh.astype(jnp.bfloat16)
         pre = jnp.dot(xn[here], w[...], preferred_element_type=jnp.float32) + bias_ref[...]
         sig = jax.nn.sigmoid(pre)
         act[here] = (pre * sig).astype(jnp.bfloat16)
-        gp[here] = (gout[here].astype(jnp.float32) * sig * (1.0 + pre * (1.0 - sig))).astype(jnp.bfloat16)
-
-    grads = lax.dot_general(xn[...], gp[...], (((0,), (0,)), ((), ())), preferred_element_type=jnp.float32)
+        grad = (gout[here].astype(jnp.float32) * sig * (1.0 + pre * (1.0 - sig))).astype(jnp.bfloat16)
+        grads += lax.dot_general(xn[here], grad, (((0,), (0,)), ((), ())), preferred_element_type=jnp.float32)
     for s in range(2):
         for m in range(32):
             r, l = F_IN * s + 8 * (m // 2), 128 * (m % 2)
@@ -264,6 +262,17 @@
             ref[8 * (m // 2):8 * (m // 2) + 8, 128 * (m % 2):128 * (m % 2) + 128] = final[s, m]
 
 
+def store(act, gs, gn, act_out, gs_out, gn_out, sem):
+    copies = [
+        pltpu.make_async_copy(src, dst, sem.at[i])
+        for i, (src, dst) in enumerate(((act, act_out), (gs, gs_out), (gn, gn_out)))
+    ]
+    for c in copies:
+        c.start()
+    for c in copies:
+        c.wait()
+
+
 def shards(mesh_shape, features, send_rows, tile_rows, tile_cols, tile_vals, w_self, w_neigh, bias, grad_out):
     rows = features.shape[0]
     tiles = tile_vals.shape[2]
@@ -281,7 +290,7 @@
         jax.ShapeDtypeStruct((F_IN, HID), f32),
         jax.ShapeDtypeStruct((F_IN, HID), f32),
     )
-    return pl.pallas_call(
+    results = pl.pallas_call(
         functools.partial(kernel, (rows, tiles, nz, ny)),
         out_shape=outs,
         in_specs=[hbm] * 9,
@@ -294,7 +303,6 @@
             pltpu.VMEM((rows, 2 * F_IN), bf16),
             pltpu.VMEM((2 * F_IN, HID), bf16),
             pltpu.VMEM((tiles, BS, BS), bf16),
-            pltpu.VMEM((rows, HID), bf16),
             pltpu.VMEM((rows, HID), bf16),
             pltpu.VMEM((nz, SEND, F_IN), f32),
             pltpu.VMEM((SEND, F_IN), f32),
@@ -318,6 +326,13 @@
         pltpu.with_memory_space_constraint(a, pltpu.HBM)
         for a in (send_rows, tile_rows, tile_cols, features, tile_vals, w_self, w_neigh, bias.reshape(1, HID), grad_out)
     ))
+    return pl.pallas_call(
+        store,
+        out_shape=outs,
+        in_specs=[vmem] * 3,
+        out_specs=(pl.BlockSpec(memory_space=pl.ANY),) * 3,
+        scratch_shapes=[dma((3,))],
+    )(*(pltpu.with_memory_space_constraint(r, pltpu.VMEM) for r in results))
 
 
 def solution(mesh):

time: 66 us -> 63.3 us (0.959)
  local copies, waits for them, and re-layouts: 2.28 us -> 0 us
    unnamed x3 -> x0, local copies, waits for them, and re-layouts: 2.28 us -> none
    pallas_call x1, Pallas kernels: 62.9 us -> 61.5 us  [shards(): pl.pallas_call(functools.partial(kernel, (rows, tiles, nz, ny)), out_shap...]
    pallas_call x0 -> x1, Pallas kernels: none -> 1.07 us  [shards(): pl.pallas_call(store, out_shape=outs, in_specs=[vmem] * 3, out_specs=(pl....]
where the time goes in v5:
time: 63.3 us; the launch traced here: 63.2 us
  Pallas kernels  62.5 us (99%)
  between operations  0.64 us (1%)
    pallas_call x1, Pallas kernels, shards(): pl.pallas_call(functools.partial(kernel, (rows, tiles, nz, ny)), out_shap...  61.5 us

profile of v5, /device:TPU:1, one launch (start us, length us, event | category | flops | bytes accessed | tf_op | source)
XLA Modules:
  0.0 63.2 jit_solution(6533709249776022631)
XLA Ops:
  0.6 61.5 %shard_map.112 = (bf16[2048,256]{1,0:T(8,128)(2,1)S(1)}, f32[128,256]{1,0:T(8,128)S(1)}, f32[128,256]{1,0:T(8,128)S(1)}) custom-call(s32[1,1,8]{2,1,0:T(1,128)} %send_hbm.1, s32[1,1,32]{2,1,0:T(1,128)} %trows_hbm.1, s32[1,1,32]{2,1,0:T(1,128)} %tcols_hbm.1, bf16[2048,128]{1,0:T(8,128)(2,1)} %feat_hbm.1, bf16[1,1,32,128,128]{4,3,2,1,0:T(8,128)(2,1)} %vals_hbm.1, ...), custom_call_target="tpu_custom_call" | custom-call | tf_op jit(solution)/shard_map/pallas_call | solution.py:293
  62.1 1.1 %shard_map.113 = (bf16[2048,256]{1,0:T(8,128)(2,1)}, f32[128,256]{1,0:T(8,128)}, f32[128,256]{1,0:T(8,128)}) custom-call(bf16[2048,256]{1,0:T(8,128)(2,1)S(1)} %get-tuple-element.6.act, f32[128,256]{1,0:T(8,128)S(1)} %get-tuple-element.7.gs, f32[128,256]{1,0:T(8,128)S(1)} %get-tuple-element.8.gn), custom_call_target="tpu_custom_call" | custom-call | tf_op jit(solution)/shard_map/pallas_call | solution.py:329

commit v6 on v5

--- a/solution.py
+++ b/solution.py
@@ -138,7 +138,7 @@
     own = place(0, 0)
     own[...] = zbuf[...].reshape(chunk, F_IN).astype(jnp.bfloat16)
 
-    far_y, near_y, all_x = (2, ny - 2, 4, 3, ny - 3), (1, ny - 1), (2, 1, NX - 1)
+    far_y, near_y, all_x = (2, ny - 2, 3, ny - 3, 4), (1, ny - 1), (2, 1, NX - 1)
 
     def send(where, sems, to):
         copy(where, where, *sems, to).start()
@@ -150,13 +150,18 @@
         send(own, (xs, xr.at[i, 0]), to_x[i])
     for k in (*far_y, *near_y):
         send(own, (ys, yr.at[k]), to_y[k])
+    for k in far_y[:4]:
+        where = place(0, -k)
+        arrived(where, yr.at[k])
+        for i in all_x:
+            send(where, (xs, xr.at[i, k]), to_x[i])
     for i in reversed(all_x):
         where = place(-i, 0)
         arrived(where, xr.at[i, 0])
         for n, k in enumerate(near_y):
             send(where, (vs, vr.at[n, i]), to_y[k])
         send(where, (cs, cr.at[i]), twin)
-    for k in far_y:
+    for k in far_y[4:]:
         where = place(0, -k)
         arrived(where, yr.at[k])
         for i in all_x:
@@ -188,10 +193,6 @@
         where = shared.at[0, pl.ds(0, chunks * chunk)]
         copy(where, where, sem, cr.at[0], twin).wait_send()
 
-    all_sent(ys, ny - 1)
-    all_sent(xs, 3 * 6)
-    all_sent(vs, 3 * 2)
-    all_sent(cs, 4 * ny)
     for i in range(NX):
         arrived(slab(1 - core, -i), cr.at[i])
 
@@ -230,6 +231,10 @@
     for i, j in plane:
         copy(half.at[x_tile[i] + yk[j]], rx_xy.at[i * ny + j - 1], ps.at[1], pr.at[1], on(i, j)).start()
     c.wait_send()
+    all_sent(ys, ny - 1)
+    all_sent(xs, 3 * 6)
+    all_sent(vs, 3 * 2)
+    all_sent(cs, 4 * ny)
     count = NX * ny - 1
     most = rx_xy.at[pl.ds(0, count)]
     copy(most, most, ps.at[1], pr.at[1], twin).wait()

time: 63.3 us -> 62.4 us (0.986)
  Pallas kernels: 62.5 us -> 61.6 us
    pallas_call x1, Pallas kernels: 61.5 us -> 60.6 us  [shards(): pl.pallas_call(functools.partial(kernel, (rows, tiles, nz, ny)), out_shap...]
where the time goes in v6:
time: 62.4 us; the launch traced here: 62.3 us
  Pallas kernels  61.6 us (99%)
  between operations  0.64 us (1%)
    pallas_call x1, Pallas kernels, shards(): pl.pallas_call(functools.partial(kernel, (rows, tiles, nz, ny)), out_shap...  60.6 us

profile of v6, /device:TPU:1, one launch (start us, length us, event | category | flops | bytes accessed | tf_op | source)
XLA Modules:
  0.0 62.3 jit_solution(1729090408369592734)
XLA Ops:
  0.6 60.6 %shard_map.112 = (bf16[2048,256]{1,0:T(8,128)(2,1)S(1)}, f32[128,256]{1,0:T(8,128)S(1)}, f32[128,256]{1,0:T(8,128)S(1)}) custom-call(s32[1,1,8]{2,1,0:T(1,128)} %send_hbm.1, s32[1,1,32]{2,1,0:T(1,128)} %trows_hbm.1, s32[1,1,32]{2,1,0:T(1,128)} %tcols_hbm.1, bf16[2048,128]{1,0:T(8,128)(2,1)} %feat_hbm.1, bf16[1,1,32,128,128]{4,3,2,1,0:T(8,128)(2,1)} %vals_hbm.1, ...), custom_call_target="tpu_custom_call" | custom-call | tf_op jit(solution)/shard_map/pallas_call | solution.py:298
  61.2 1.1 %shard_map.113 = (bf16[2048,256]{1,0:T(8,128)(2,1)}, f32[128,256]{1,0:T(8,128)}, f32[128,256]{1,0:T(8,128)}) custom-call(bf16[2048,256]{1,0:T(8,128)(2,1)S(1)} %get-tuple-element.6.act, f32[128,256]{1,0:T(8,128)S(1)} %get-tuple-element.7.gs, f32[128,256]{1,0:T(8,128)S(1)} %get-tuple-element.8.gn), custom_call_target="tpu_custom_call" | custom-call | tf_op jit(solution)/shard_map/pallas_call | solution.py:334

commit v7 on v6

--- a/solution.py
+++ b/solution.py
@@ -199,11 +199,7 @@
     for t in range(tiles):
         here = pl.ds(tile_cols[0, 0, t] * 64, 64)
         taken = jnp.concatenate([shared[0, here], shared[1, here]], axis=0)
-        prods[t + 1] = jnp.dot(vals[t], taken, preferred_element_type=jnp.float32)
-
-    @pl.loop(0, tiles)
-    def _(t):
-        prods[t + 1] = prods[t + 1] + prods[links[t]]
+        prods[t + 1] = jnp.dot(vals[t], taken, preferred_element_type=jnp.float32) + prods[links[t]]
 
     step_rows = 4 * BS
     grads = jnp.zeros((2 * F_IN, HID), jnp.float32)

time: 62.4 us -> 62.1 us (level)
  no operation moved by 1% of the time
where the time goes in v7:
time: 62.1 us; the launch traced here: 61.9 us
  Pallas kernels  61.3 us (99%)
  between operations  0.64 us (1%)
    pallas_call x1, Pallas kernels, shards(): pl.pallas_call(functools.partial(kernel, (rows, tiles, nz, ny)), out_shap...  60.2 us

profile of v7, /device:TPU:1, one launch (start us, length us, event | category | flops | bytes accessed | tf_op | source)
XLA Modules:
  0.0 61.9 jit_solution(1378468773730768887)
XLA Ops:
  0.6 60.2 %shard_map.112 = (bf16[2048,256]{1,0:T(8,128)(2,1)S(1)}, f32[128,256]{1,0:T(8,128)S(1)}, f32[128,256]{1,0:T(8,128)S(1)}) custom-call(s32[1,1,8]{2,1,0:T(1,128)} %send_hbm.1, s32[1,1,32]{2,1,0:T(1,128)} %trows_hbm.1, s32[1,1,32]{2,1,0:T(1,128)} %tcols_hbm.1, bf16[2048,128]{1,0:T(8,128)(2,1)} %feat_hbm.1, bf16[1,1,32,128,128]{4,3,2,1,0:T(8,128)(2,1)} %vals_hbm.1, ...), custom_call_target="tpu_custom_call" | custom-call | tf_op jit(solution)/shard_map/pallas_call | solution.py:294
  60.8 1.1 %shard_map.113 = (bf16[2048,256]{1,0:T(8,128)(2,1)}, f32[128,256]{1,0:T(8,128)}, f32[128,256]{1,0:T(8,128)}) custom-call(bf16[2048,256]{1,0:T(8,128)(2,1)S(1)} %get-tuple-element.6.act, f32[128,256]{1,0:T(8,128)S(1)} %get-tuple-element.7.gs, f32[128,256]{1,0:T(8,128)S(1)} %get-tuple-element.8.gn), custom_call_target="tpu_custom_call" | custom-call | tf_op jit(solution)/shard_map/pallas_call | solution.py:330
